TPU v7x, 1024 devices: a whole 8x8x8 slice. The times are simulated.
1024 devices in a mesh: rows: 64 (over y, z), cols: 16 (over x, core).
Axes of the slice: x: 8, y: 8, z: 8, core: 2. Of those that a mesh axis runs over, the one named last changes fastest.
Arguments:
- hamiltonian: float32 [256, 8, 128, 128], P('rows'), may hold values from -6 to 6
- intersection_root: float32 [256, 8, 128, 128], P('rows'), may hold values from -0.1875 to 0.1875
- ham_pattern: int32 [256, 8], replicated, may hold values from -1 to 255, as said below
- root_pattern: int32 [256, 8], replicated, may hold values from -1 to 255, as said below
- filter_pattern: int32 [256, 8], replicated, may hold values from -1 to 255, as said below
Outputs:
- projected: float32 [256, 8, 128, 128], P('rows', None, 'cols')
Inputs may be any that keep to these rules, and one draw needn't show every extreme that they name: `ham_pattern`: in every row i the used slots come first and hold distinct block columns, all within 4 block rows of i counted cyclically over the 256 block rows; slot 0 holds i itself; every row uses 2 or more slots and some row uses all 8. `root_pattern`: same rules as ham_pattern, drawn independently. `filter_pattern`: same rules as ham_pattern, drawn independently.
All inputs are finite; a program needn't handle non-finite values.
Results may differ from a plain program's by a relative error of at most 0.0003.
Values sent between devices are 32-bit elements; how exact they have to be, the bound alone decides.
A program may use at most 32 MiB of HBM per device.

v0:
```python
import jax
import jax.numpy as jnp
from jax import lax
from jax.sharding import PartitionSpec as P

REACH = 4


HIGHEST_ACCURACY = lax.Precision.HIGHEST


def padded(cells, sides, width):
    for axis, dim in sides:
        count = lax.axis_size(axis)
        head = lax.slice_in_dim(cells, 0, width, axis=dim)
        tail = lax.slice_in_dim(cells, cells.shape[dim] - width, cells.shape[dim], axis=dim)
        cells = jnp.concatenate(
            [
                lax.ppermute(tail, axis, [(i, (i + 1) % count) for i in range(count)]),
                cells,
                lax.ppermute(head, axis, [((i + 1) % count, i) for i in range(count)]),
            ],
            axis=dim,
        )
    return cells


def shifted(x, axis, by):
    devices = lax.axis_size(axis)
    return lax.ppermute(x, axis, [(i, (i + by) % devices) for i in range(devices)])


def slice_window(local_slices):
    return padded(local_slices, (("rows", 0),), REACH)


def select_right(row_window, right_pattern, left_columns, out_columns, first_row, total_rows):
    usable = left_columns >= 0
    safe_columns = jnp.where(usable, left_columns, 0)
    position = jnp.where(usable, jnp.mod(safe_columns - first_row, total_rows), 0)
    picked = row_window[position]
    picked_columns = right_pattern[safe_columns]
    matches = (
        (picked_columns[:, :, :, None] == out_columns[:, None, None, :])
        & (out_columns[:, None, None, :] >= 0)
        & usable[:, :, None, None]
    )
    return jnp.einsum(
        "ksut,ksucb->kstcb", matches.astype(jnp.float32), picked, precision=HIGHEST_ACCURACY
    )


def shards(hamiltonian, intersection_root, ham_pattern, root_pattern, filter_pattern):
    local_rows = hamiltonian.shape[0]
    total_rows = ham_pattern.shape[0]
    block_width = hamiltonian.shape[2]
    slice_width = block_width // lax.axis_size("cols")
    first_local = lax.axis_index("rows") * local_rows
    first_row = first_local - REACH
    ham_local = lax.dynamic_slice_in_dim(ham_pattern, first_local, local_rows, 0)
    root_local = lax.dynamic_slice_in_dim(root_pattern, first_local, local_rows, 0)
    filter_local = lax.dynamic_slice_in_dim(filter_pattern, first_local, local_rows, 0)
    root_slices = jnp.swapaxes(
        lax.dynamic_slice_in_dim(
            intersection_root, lax.axis_index("cols") * slice_width, slice_width, 3
        ),
        2,
        3,
    )
    selected_blocks = select_right(
        slice_window(root_slices), root_pattern, ham_local, filter_local, first_row, total_rows
    )
    product = jnp.einsum(
        "kstcb,ksab->ktca", selected_blocks, hamiltonian, precision=HIGHEST_ACCURACY
    )
    usable = root_local >= 0
    safe_columns = jnp.where(usable, root_local, 0)
    target_columns = filter_pattern[safe_columns]
    matches = (
        (filter_local[:, None, :, None] == target_columns[:, :, None, :])
        & (target_columns[:, :, None, :] >= 0)
        & usable[:, :, None, None]
    )
    picked = jnp.einsum(
        "ksut,kucb->kstcb", matches.astype(jnp.float32), product, precision=HIGHEST_ACCURACY
    )
    contributions = jnp.einsum(
        "kstcb,ksba->kstca", picked, intersection_root, precision=HIGHEST_ACCURACY
    )
    position = jnp.mod(safe_columns - first_row, total_rows)
    window_row_block = local_rows + 2 * REACH
    onehot = (
        (position[:, :, None] == jnp.arange(window_row_block, dtype=jnp.int32)[None, None, :])
        & usable[:, :, None]
    ).astype(jnp.float32)
    partial_value = jnp.einsum("ksw,kstca->wtca", onehot, contributions, precision=HIGHEST_ACCURACY)
    lower_rim = partial_value[:REACH]
    upper_rim = partial_value[REACH + local_rows :]
    from_below = shifted(upper_rim, "rows", 1)
    from_above = shifted(lower_rim, "rows", -1)
    filler = jnp.zeros((local_rows - REACH,) + partial_value.shape[1:], jnp.float32)
    assembled = (
        partial_value[REACH : REACH + local_rows]
        + jnp.concatenate([from_below, filler], 0)
        + jnp.concatenate([filler, from_above], 0)
    )
    selected_blocks = select_right(
        slice_window(assembled), filter_pattern, filter_local, filter_local, first_row, total_rows
    )
    gathered = lax.all_gather(assembled, "cols", axis=2, tiled=True)
    square = jnp.einsum("kstcb,ksba->ktca", selected_blocks, gathered, precision=HIGHEST_ACCURACY)
    purified = 2.0 * assembled - square
    selected_blocks = select_right(
        slice_window(purified), filter_pattern, root_local, filter_local, first_row, total_rows
    )
    return jnp.einsum(
        "kstcb,ksab->ktca", selected_blocks, intersection_root, precision=HIGHEST_ACCURACY
    )


def solution(mesh):
    return jax.shard_map(
        shards,
        mesh=mesh,
        in_specs=(P("rows", None, None, None), P("rows", None, None, None), P(), P(), P()),
        out_specs=P("rows", None, "cols", None),
        check_vma=False,
    )
```

profile of v0, /device:TPU:1, one launch (start us, length us, event | category | flops | bytes accessed | tf_op | source)
XLA Modules:
  0.0 135.3 jit_solution(12369657780659425260)
XLA Ops:
  6.5 1.6 %copy-done = f32[4,8,128,128]{3,2,1,0:T(8,128)S(1)} copy-done((f32[4,8,128,128]{3,2,1,0:T(8,128)S(1)}, f32[4,8,128,128]{3,2,1,0:T(8,128)}, u32[]{:S(2)}) %copy-start) | copy-done | bytes 2097176
  8.1 2.0 %constant_dynamic-slice_fusion = f32[4,8,128,8]{3,2,1,0:T(8,128)} fusion(f32[4,8,128,128]{3,2,1,0:T(8,128)S(1)} %copy-done, s32[]{:T(128)S(6)} %select_n.70), kind=kLoop, calls=%fused_computation.102 | loop fusion | bytes 262148 | tf_op jit(solution)/shard_map/dynamic_slice | solution.py:64
  10.1 2.2 %copy.105 = f32[4,8,128,8]{2,3,1,0:T(8,128)S(1)} copy(f32[4,8,128,8]{3,2,1,0:T(8,128)} %constant_dynamic-slice_fusion) | data formatting | bytes 262144
  12.3 5.7 %collective-permute-start = (f32[4,8,8,128]{3,2,1,0:T(8,128)S(1)}, f32[4,8,8,128]{3,2,1,0:T(8,128)S(1)}, u32[]{:S(2)}, u32[]{:S(2)}) collective-permute-start(f32[4,8,8,128]{3,2,1,0:T(8,128)S(1)} %bitcast.86), channel_id=1, source_target_pairs={{0,16},{16,32},{32,48},{48,64},{64,80},{80,96},{96,112},{112,128},... | collective-permute-start | bytes 393224 | tf_op jit(solution)/shard_map/ppermute | solution.py:19
  18.0 17.7 %collective-permute-start.1 = (f32[4,8,8,128]{3,2,1,0:T(8,128)S(1)}, f32[4,8,8,128]{3,2,1,0:T(8,128)S(1)}, u32[]{:S(2)}, u32[]{:S(2)}) collective-permute-start(f32[4,8,8,128]{3,2,1,0:T(8,128)S(1)} %bitcast.87), channel_id=1, source_target_pairs={{16,0},{32,16},{48,32},{64,48},{80,64},{96,80},{112,96},{128,112},... | collective-permute-start | bytes 393224 | tf_op jit(solution)/shard_map/ppermute | solution.py:21
  42.0 1.2 gather_fusion.1
  44.6 1.6 %fusion.20 = f32[4,8,8,8,128]{4,2,3,1,0:T(8,128)S(1)} fusion(f32[4,8,8,8,128]{4,3,2,1,0:T(8,128)S(1)} %bitcast.83, s32[4,8,8]{2,1,0:T(8,128)} %bitcast.91, s32[4,8]{1,0:T(4,128)} %copy.48, pred[4,8]{1,0:T(4,128)(4,1)} %copy.56, pred[4,8]{1,0:T(4,128)(4,1)} %copy.49), kind=kOutput, calls=%fused_computation.23 | convolution fusion | flops 25171968 | bytes 2098368 | tf_op jit(solution)/shard_map/ksut,ksucb->kstcb/dot_general | solution.py:48
  46.2 2.3 %fusion = f32[4,8,8,128,1]{3,1,2,4,0:T(8,128)S(1)} fusion(f32[4,8,8,8,128]{4,2,3,1,0:T(8,128)S(1)} %fusion.20, f32[4,8,128,128]{3,2,1,0:T(8,128)S(1)} %copy-done.2), kind=kOutput, calls=%fused_computation.6 | convolution fusion | flops 402653184 | bytes 3276800 | tf_op jit(solution)/shard_map/kstcb,ksab->ktca/dot_general | solution.py:73
  49.2 2.0 %fusion.6 = f32[4,8,8,8,128]{4,2,3,1,0:T(8,128)S(1)} fusion(f32[4,8,8,8,128]{4,2,3,1,0:T(8,128)S(1)} %fusion.25, f32[4,8,128,128]{3,2,1,0:T(8,128)S(1)} %copy-done), kind=kOutput, calls=%fused_computation.12 | convolution fusion | flops 402653184 | bytes 4194304 | tf_op jit(solution)/shard_map/kstcb,ksba->kstca/dot_general | solution.py:87
  51.3 1.1 convolution_bitcast_fusion
  52.4 1.9 %collective-permute-start.2 = (f32[4,8,8,128]{3,0,2,1:T(4,128)S(1)}, f32[4,8,8,128]{3,0,2,1:T(4,128)S(1)}, u32[]{:S(2)}, u32[]{:S(2)}) collective-permute-start(f32[4,8,8,128]{3,0,2,1:T(4,128)S(1)} %get-tuple-element.12), channel_id=1, source_target_pairs={{0,16},{16,32},{32,48},{48,64},{64,80},{80,96},{96,112},{112,128},... | collective-permute-start | bytes 393224 | tf_op jit(solution)/shard_map/ppermute | solution.py:30
  54.4 6.7 %collective-permute-start.3 = (f32[4,8,8,128]{3,0,2,1:T(4,128)S(1)}, f32[4,8,8,128]{3,0,2,1:T(4,128)S(1)}, u32[]{:S(2)}, u32[]{:S(2)}) collective-permute-start(f32[4,8,8,128]{3,0,2,1:T(4,128)S(1)} %get-tuple-element.13), channel_id=1, source_target_pairs={{0,1008},{16,0},{32,16},{48,32},{64,48},{80,64},{96,80},{112,96},{... | collective-permute-start | bytes 393224 | tf_op jit(solution)/shard_map/ppermute | solution.py:30
  61.5 1.5 %collective-permute-done.3 = f32[4,8,8,128]{3,0,2,1:T(4,128)S(1)} collective-permute-done((f32[4,8,8,128]{3,0,2,1:T(4,128)S(1)}, f32[4,8,8,128]{3,0,2,1:T(4,128)S(1)}, u32[]{:S(2)}, u32[]{:S(2)}) %collective-permute-start.3) | collective-permute-done | bytes 131104 | tf_op jit(solution)/shard_map/ppermute | solution.py:30
  63.9 1.9 %collective-permute-start.4 = (f32[4,8,8,128]{3,0,2,1:T(4,128)}, f32[4,8,8,128]{3,0,2,1:T(4,128)S(1)}, u32[]{:S(2)}, u32[]{:S(2)}) collective-permute-start(f32[4,8,8,128]{3,0,2,1:T(4,128)} %fusion.22), channel_id=1, source_target_pairs={{0,16},{16,32},{32,48},{48,64},{64,80},{80,96},{96,112},{112,128},... | collective-permute-start | bytes 393224 | tf_op jit(solution)/shard_map/ppermute | solution.py:19
  65.9 7.1 %collective-permute-start.5 = (f32[4,8,8,128]{3,0,2,1:T(4,128)}, f32[4,8,8,128]{3,0,2,1:T(4,128)S(1)}, u32[]{:S(2)}, u32[]{:S(2)}) collective-permute-start(f32[4,8,8,128]{3,0,2,1:T(4,128)} %fusion.22), channel_id=1, source_target_pairs={{16,0},{32,16},{48,32},{64,48},{80,64},{96,80},{112,96},{128,112},... | collective-permute-start | bytes 393224 | tf_op jit(solution)/shard_map/ppermute | solution.py:21
  73.7 1.5 %collective-permute-done.5 = f32[4,8,8,128]{3,0,2,1:T(4,128)S(1)} collective-permute-done((f32[4,8,8,128]{3,0,2,1:T(4,128)}, f32[4,8,8,128]{3,0,2,1:T(4,128)S(1)}, u32[]{:S(2)}, u32[]{:S(2)}) %collective-permute-start.5) | collective-permute-done | bytes 131104 | tf_op jit(solution)/shard_map/ppermute | solution.py:21
  76.3 1.6 %gather_fusion.4 = f32[32,8,8,128]{3,2,1,0:T(8,128)} fusion(f32[12,8,8,128]{3,2,1,0:T(8,128)S(1)} %copy.68, s32[1024]{0:T(1024)S(1)} %pad_clamp_fusion.1), kind=kCustom, calls=%fused_computation.4 | custom fusion | bytes 2097280 | tf_op jit(solution)/shard_map/gather | solution.py:41
  77.9 1.9 %fusion.18 = f32[4,8,8,8,128]{4,2,3,1,0:T(8,128)S(1)} fusion(f32[4,8,8,8,128]{4,3,2,1,0:T(8,128)} %bitcast.84, s32[4,8,8]{2,1,0:T(8,128)S(1)} %bitcast.92, s32[4,8]{1,0:T(4,128)S(1)} %copy-done.7, pred[4,8]{1,0:T(4,128)(4,1)S(1)} %copy-done.13), kind=kOutput, calls=%fused_computation.21 | convolution fusion | flops 25171968 | bytes 2098336 | tf_op jit(solution)/shard_map/ksut,ksucb->kstcb/dot_general | solution.py:48
  79.9 26.2 %all-gather.2.cloned.1.call-done = f32[4,8,128,128]{3,0,2,1:T(4,128)} async-done(((f32[4,8,8,128]{3,0,2,1:T(4,128)}), f32[4,8,128,128]{3,0,2,1:T(4,128)}) %all-gather.2.cloned.1.call-update) | async-done | bytes 2097168 | tf_op jit(solution)/shard_map/all_gather | solution.py:110
  106.1 3.0 %fusion.12 = f32[4,8,8,128]{3,1,2,0:T(8,128)S(1)} fusion(f32[4,8,8,8,128]{4,2,3,1,0:T(8,128)S(1)} %fusion.18, f32[4,8,128,128,1]{3,0,2,1,4:T(4,128)} %bitcast.85), kind=kOutput, calls=%fused_computation.17 | convolution fusion | flops 402653184 | bytes 3276800 | tf_op jit(solution)/shard_map/kstcb,ksba->ktca/dot_general | solution.py:111
  109.2 3.5 %collective-permute-start.6 = (f32[4,8,8,128]{3,0,2,1:T(4,128)S(1)}, f32[4,8,8,128]{3,0,2,1:T(4,128)S(1)}, u32[]{:S(2)}, u32[]{:S(2)}) collective-permute-start(f32[4,8,8,128]{3,0,2,1:T(4,128)S(1)} %copy_subtract_fusion), channel_id=1, source_target_pairs={{0,16},{16,32},{32,48},{48,64},{64,80},{80,96},{96,112},{112,128},... | collective-permute-start | bytes 393224 | tf_op jit(solution)/shard_map/ppermute | solution.py:19
  112.7 7.9 %collective-permute-start.7 = (f32[4,8,8,128]{3,0,2,1:T(4,128)S(1)}, f32[4,8,8,128]{3,0,2,1:T(4,128)S(1)}, u32[]{:S(2)}, u32[]{:S(2)}) collective-permute-start(f32[4,8,8,128]{3,0,2,1:T(4,128)S(1)} %copy_subtract_fusion), channel_id=1, source_target_pairs={{16,0},{32,16},{48,32},{64,48},{80,64},{96,80},{112,96},{128,112},... | collective-permute-start | bytes 393224 | tf_op jit(solution)/shard_map/ppermute | solution.py:21
  124.1 1.4 %fusion.16 = f32[4,8,8,8,128]{4,2,3,1,0:T(8,128)S(1)} fusion(f32[4,8,8,8,128]{4,3,2,1,0:T(8,128)S(1)} %bitcast.82, s32[4,8]{1,0:T(4,128)} %copy.48, s32[4,8,8]{2,1,0:T(8,128)S(1)} %bitcast.90, pred[4,8]{1,0:T(4,128)(4,1)} %copy.50, pred[4,8]{1,0:T(4,128)(4,1)} %copy.49), kind=kOutput, calls=%fused_computation.19 | convolution fusion | flops 25171968 | bytes 2098368 | tf_op jit(solution)/shard_map/ksut,ksucb->kstcb/dot_general | solution.py:48
  125.5 2.3 %fusion.9 = f32[4,8,8,128,1]{3,1,4,2,0:T(8,128)S(1)} fusion(f32[4,8,8,8,128]{4,2,3,1,0:T(8,128)S(1)} %fusion.16, f32[4,8,128,128]{3,2,1,0:T(8,128)S(1)} %copy-done), kind=kOutput, calls=%fused_computation.16 | convolution fusion | flops 402653184 | bytes 3276800 | tf_op jit(solution)/shard_map/kstcb,ksab->ktca/dot_general | solution.py:116
  (87 shorter events, 15.7 us)
Async XLA Ops:
  6.5 99.5 %all-gather.2.cloned.1.call-start = ((), (), s32[]{:S(2)}) async-start(), calls=%async_computation | async-start | bytes 2228224 | tf_op jit(solution)/shard_map/all_gather | solution.py:110
  10.1 25.7 %copy-start.9 = (s32[256,8]{0,1:T(8,128)S(1)}, s32[256,8]{0,1:T(8,128)}, u32[]{:S(2)}) copy-start(s32[256,8]{0,1:T(8,128)} %param.9) | copy-start | bytes 24580
  10.1 25.9 %copy-start.15 = (s32[256,8]{0,1:T(8,128)S(1)}, s32[256,8]{0,1:T(8,128)}, u32[]{:S(2)}) copy-start(s32[256,8]{0,1:T(8,128)} %param.7) | copy-start | bytes 24580
  10.1 26.0 %copy-start.8 = (s32[256,8]{0,1:T(8,128)S(1)}, s32[256,8]{0,1:T(8,128)}, u32[]{:S(2)}) copy-start(s32[256,8]{0,1:T(8,128)} %param.8) | copy-start | bytes 24580
  12.3 31.5 %collective-permute-start = (f32[4,8,8,128]{3,2,1,0:T(8,128)S(1)}, f32[4,8,8,128]{3,2,1,0:T(8,128)S(1)}, u32[]{:S(2)}, u32[]{:S(2)}) collective-permute-start(f32[4,8,8,128]{3,2,1,0:T(8,128)S(1)} %bitcast.86), channel_id=1, source_target_pairs={{0,16},{16,32},{32,48},{48,64},{64,80},{80,96},{96,112},{112,128},... | collective-permute-start | bytes 393224 | tf_op jit(solution)/shard_map/ppermute | solution.py:19
  18.0 25.8 %collective-permute-start.1 = (f32[4,8,8,128]{3,2,1,0:T(8,128)S(1)}, f32[4,8,8,128]{3,2,1,0:T(8,128)S(1)}, u32[]{:S(2)}, u32[]{:S(2)}) collective-permute-start(f32[4,8,8,128]{3,2,1,0:T(8,128)S(1)} %bitcast.87), channel_id=1, source_target_pairs={{16,0},{32,16},{48,32},{64,48},{80,64},{96,80},{112,96},{128,112},... | collective-permute-start | bytes 393224 | tf_op jit(solution)/shard_map/ppermute | solution.py:21
  35.9 7.9 %copy-start.3 = (s32[256,8]{1,0:T(8,128)}, s32[256,8]{1,0:T(8,128)S(1)}, u32[]{:S(2)}) copy-start(s32[256,8]{1,0:T(8,128)S(1)} %copy.47) | copy-start | bytes 24580
  36.8 2.3 %copy-start.5 = (s32[4,8]{0,1:T(8,128)}, s32[4,8]{0,1:T(8,128)S(1)}, u32[]{:S(2)}) copy-start(s32[4,8]{0,1:T(8,128)S(1)} %get-tuple-element.15) | copy-start | bytes 388
  46.2 2.3 %copy-start.7 = (s32[4,8]{1,0:T(4,128)S(1)}, s32[4,8]{1,0:T(4,128)}, u32[]{:S(2)}) copy-start(s32[4,8]{1,0:T(4,128)} %copy.48) | copy-start | bytes 388
  46.2 2.3 %copy-start.10 = (pred[4,8,8]{2,1,0:T(8,128)(4,1)S(1)}, pred[4,8,8]{2,1,0:T(8,128)(4,1)}, u32[]{:S(2)}) copy-start(pred[4,8,8]{2,1,0:T(8,128)(4,1)} %broadcast_compare_fusion) | copy-start | bytes 772
  46.2 2.3 %copy-start.16 = (pred[4,8]{1,0:T(4,128)(4,1)S(1)}, pred[4,8]{1,0:T(4,128)(4,1)}, u32[]{:S(2)}) copy-start(pred[4,8]{1,0:T(4,128)(4,1)} %copy.50) | copy-start | bytes 100
  49.2 2.0 %copy-start.14 = (s32[4,8]{1,0:T(4,128)S(1)}, s32[4,8]{1,0:T(4,128)}, u32[]{:S(2)}) copy-start(s32[4,8]{1,0:T(4,128)} %copy.51) | copy-start | bytes 388
  51.2 12.5 %copy-start.12 = (s32[4,8]{0,1:T(8,128)S(1)}, s32[4,8]{0,1:T(8,128)}, u32[]{:S(2)}) copy-start(s32[4,8]{0,1:T(8,128)} %get-tuple-element.14) | copy-start | bytes 388
  51.2 12.7 %copy-start.6 = (s32[4,8]{0,1:T(8,128)S(1)}, s32[4,8]{0,1:T(8,128)}, u32[]{:S(2)}) copy-start(s32[4,8]{0,1:T(8,128)} %copy-done.5) | copy-start | bytes 388
  51.2 21.9 %copy-start.4 = (s32[256,8]{1,0:T(8,128)S(1)}, s32[256,8]{1,0:T(8,128)}, u32[]{:S(2)}) copy-start(s32[256,8]{1,0:T(8,128)} %copy-done.3) | copy-start | bytes 24580
  52.4 9.0 %collective-permute-start.2 = (f32[4,8,8,128]{3,0,2,1:T(4,128)S(1)}, f32[4,8,8,128]{3,0,2,1:T(4,128)S(1)}, u32[]{:S(2)}, u32[]{:S(2)}) collective-permute-start(f32[4,8,8,128]{3,0,2,1:T(4,128)S(1)} %get-tuple-element.12), channel_id=1, source_target_pairs={{0,16},{16,32},{32,48},{48,64},{64,80},{80,96},{96,112},{112,128},... | collective-permute-start | bytes 393224 | tf_op jit(solution)/shard_map/ppermute | solution.py:30
  54.4 8.6 %collective-permute-start.3 = (f32[4,8,8,128]{3,0,2,1:T(4,128)S(1)}, f32[4,8,8,128]{3,0,2,1:T(4,128)S(1)}, u32[]{:S(2)}, u32[]{:S(2)}) collective-permute-start(f32[4,8,8,128]{3,0,2,1:T(4,128)S(1)} %get-tuple-element.13), channel_id=1, source_target_pairs={{0,1008},{16,0},{32,16},{48,32},{64,48},{80,64},{96,80},{112,96},{... | collective-permute-start | bytes 393224 | tf_op jit(solution)/shard_map/ppermute | solution.py:30
  63.7 14.2 %copy-start.13 = (pred[4,8]{1,0:T(4,128)(4,1)S(1)}, pred[4,8]{1,0:T(4,128)(4,1)}, u32[]{:S(2)}) copy-start(pred[4,8]{1,0:T(4,128)(4,1)} %copy.49) | copy-start | bytes 100
  63.9 9.8 %collective-permute-start.4 = (f32[4,8,8,128]{3,0,2,1:T(4,128)}, f32[4,8,8,128]{3,0,2,1:T(4,128)S(1)}, u32[]{:S(2)}, u32[]{:S(2)}) collective-permute-start(f32[4,8,8,128]{3,0,2,1:T(4,128)} %fusion.22), channel_id=1, source_target_pairs={{0,16},{16,32},{32,48},{48,64},{64,80},{80,96},{96,112},{112,128},... | collective-permute-start | bytes 393224 | tf_op jit(solution)/shard_map/ppermute | solution.py:19
  65.9 9.3 %collective-permute-start.5 = (f32[4,8,8,128]{3,0,2,1:T(4,128)}, f32[4,8,8,128]{3,0,2,1:T(4,128)S(1)}, u32[]{:S(2)}, u32[]{:S(2)}) collective-permute-start(f32[4,8,8,128]{3,0,2,1:T(4,128)} %fusion.22), channel_id=1, source_target_pairs={{16,0},{32,16},{48,32},{64,48},{80,64},{96,80},{112,96},{128,112},... | collective-permute-start | bytes 393224 | tf_op jit(solution)/shard_map/ppermute | solution.py:21
  79.9 29.2 %copy-start.1 = (f32[4,8,8,128]{3,0,2,1:T(4,128)S(1)}, f32[4,8,8,128]{3,0,2,1:T(4,128)}, u32[]{:S(2)}) copy-start(f32[4,8,8,128]{3,0,2,1:T(4,128)} %fusion.22) | copy-start | bytes 393220
  79.9 40.8 %copy-start.11 = (s32[4,8]{0,1:T(8,128)S(1)}, s32[4,8]{0,1:T(8,128)}, u32[]{:S(2)}) copy-start(s32[4,8]{0,1:T(8,128)} %get-tuple-element.5) | copy-start | bytes 388
  109.2 13.0 %collective-permute-start.6 = (f32[4,8,8,128]{3,0,2,1:T(4,128)S(1)}, f32[4,8,8,128]{3,0,2,1:T(4,128)S(1)}, u32[]{:S(2)}, u32[]{:S(2)}) collective-permute-start(f32[4,8,8,128]{3,0,2,1:T(4,128)S(1)} %copy_subtract_fusion), channel_id=1, source_target_pairs={{0,16},{16,32},{32,48},{48,64},{64,80},{80,96},{96,112},{112,128},... | collective-permute-start | bytes 393224 | tf_op jit(solution)/shard_map/ppermute | solution.py:19
  112.7 10.4 %collective-permute-start.7 = (f32[4,8,8,128]{3,0,2,1:T(4,128)S(1)}, f32[4,8,8,128]{3,0,2,1:T(4,128)S(1)}, u32[]{:S(2)}, u32[]{:S(2)}) collective-permute-start(f32[4,8,8,128]{3,0,2,1:T(4,128)S(1)} %copy_subtract_fusion), channel_id=1, source_target_pairs={{16,0},{32,16},{48,32},{64,48},{80,64},{96,80},{112,96},{128,112},... | collective-permute-start | bytes 393224 | tf_op jit(solution)/shard_map/ppermute | solution.py:21
  (2 other events, 3.2 us)
Sparse Core Ops, SparseCore 0:
  63.8 42.1 all-gather.1
where the time goes:
time: 136 us; the launch traced here: 135 us
  starting transfers between devices  52.5 us (39%)
  waiting for transfers between devices  31.3 us (23%)
  local copies, waits for them, and re-layouts  16.8 us (12%)
  matrix products  16.3 us (12%)
  between operations  13.8 us (10%)
  other arithmetic  4.69 us (3%)
    ppermute x3, starting transfers between devices, padded(): lax.ppermute(head, axis, [((i + 1) % count, i) for i in range(count)])  32.8 us
    all_gather x1, waiting for transfers between devices, shards(): gathered = lax.all_gather(assembled, 'cols', axis=2, tiled=True)  26.2 us
    ppermute x3, starting transfers between devices, padded(): lax.ppermute(tail, axis, [(i, (i + 1) % count) for i in range(count)])  11.1 us
    ppermute x2, starting transfers between devices, shifted(): lax.ppermute(x, axis, [(i, (i + by) % devices) for i in range(devices)])  8.6 us
    dot_general x3, matrix products, select_right(): jnp.einsum('ksut,ksucb->kstcb', matches.astype(jnp.float32), picked, prec...  4.91 us
    unnamed x37, local copies, waits for them, and re-layouts  4.11 us
    gather x3, local copies, waits for them, and re-layouts, select_right(): picked = row_window[position]  3.07 us
    dot_general x1, matrix products, shards(): jnp.einsum('kstcb,ksba->ktca', selected_blocks, gathered, precision=HIGHE...  3.01 us
  transfers between devices with their start and end apart: 9, of which 6 were waited for; matrix products, arithmetic and copies ran while one was open for 11% of the time, Pallas kernels for 0%

commit v1 on v0

v1 whole, which is shorter than its diff:
```python
import functools

import jax
import jax.numpy as jnp
from jax import lax
from jax.experimental import pallas as pl
from jax.experimental.pallas import tpu as pltpu
from jax.sharding import PartitionSpec as P

R = 4
K = 8
N = 128
C = 8
BAND = 2 * R + 1
WIN = 3 * R
CHIPS = 8
F32, BF16 = jnp.float32, jnp.bfloat16


def split(x):
    hi = x.astype(BF16).astype(F32)
    return hi, x - hi


def stacked(x):
    return jnp.concatenate(split(x), 0).astype(BF16)


def rows_of(tiles):
    return tiles.reshape(tiles.shape[0] * C, N)


def quadrants(x):
    half = x.shape[0] // 2
    return (x[half:, N:] + x[half:, :N]) + (x[:half, N:] + x[:half, :N])


def dot(a, b, b_dim):
    return lax.dot_general(a, b, (((1,), (b_dim,)), ((), ())), preferred_element_type=F32)


def kernel(
    total_rows, h_hbm, z_hbm, hp_hbm, rp_hbm, fp_hbm, out,
    hp, rp, fp, zbuf, hbuf, hsplit, zsplit, merged, zslot, zwin, wband, part, from_next, from_prev,
    xwin, xband, xall, lefts, pwin, yband,
    load_sem, pat_sem, halo_send, halo_recv, part_send, part_recv, ring_send, ring_recv, pair_send, pair_recv,
):
    groups = total_rows // R
    row, col = lax.axis_index("rows"), lax.axis_index("cols")
    chip, core = col // 2, lax.rem(col, 2)
    first = row * R
    nxt = {"rows": lax.rem(row + 1, groups), "cols": col}
    prv = {"rows": lax.rem(row + groups - 1, groups), "cols": col}
    right = {"rows": row, "cols": lax.rem(chip + 1, CHIPS) * 2 + core}
    left = {"rows": row, "cols": lax.rem(chip + CHIPS - 1, CHIPS) * 2 + core}
    other = {"rows": row, "cols": chip * 2 + (1 - core)}

    pats = [
        pltpu.make_async_copy(a, b, pat_sem.at[i])
        for i, (a, b) in enumerate(((rp_hbm, rp), (hp_hbm, hp), (fp_hbm, fp)))
    ]
    zloads = [pltpu.make_async_copy(z_hbm.at[k], zbuf.at[k], load_sem.at[0, k]) for k in range(R)]
    hloads = [pltpu.make_async_copy(h_hbm.at[k], hbuf.at[k], load_sem.at[1, k]) for k in range(R)]
    for c in pats + zloads + hloads:
        c.start()

    with jax.named_scope("zeros"):
        for win in (zwin, xwin, pwin):
            for r in range(WIN + 1):
                win[r] = jnp.zeros((WIN + 1, C, N), F32)
        for k in range(R):
            wband[k] = jnp.zeros((WIN, C, N), F32)
            yband[k] = jnp.zeros((WIN + 1, C, N), F32)
            xband[k, WIN] = jnp.zeros((C, N), F32)
            zslot[k, K] = jnp.zeros((C, N), F32)
            zsplit[k, K] = jnp.zeros((N, 2 * N), BF16)

    barrier = pltpu.get_barrier_semaphore()
    for device in (nxt, prv, right, left, other):
        pl.semaphore_signal(barrier, inc=1, device_id=device, device_id_type=pl.DeviceIdType.MESH)

    for c in pats:
        c.wait()

    def relative(pat, i, s):
        p = pat[s, first + i]
        v = p - first + R
        v = jnp.where(v < 0, v + total_rows, v)
        v = jnp.where(v >= total_rows, v - total_rows, v)
        return jnp.where(p < 0, WIN, jnp.minimum(v, WIN))

    def slot_at(rel, i, d):
        slot = jnp.int32(K)
        for s in range(K):
            slot = jnp.where(rel[i][s] == i + d, s, slot)
        return slot

    with jax.named_scope("root tables"):
        rrel = [[relative(rp, i, s) for s in range(K)] for i in range(R)]
        zslots = [[slot_at(rrel, i, d) for d in range(BAND)] for i in range(R)]

    lane = lax.broadcasted_iota(jnp.int32, (N, N), 1) // C
    with jax.named_scope("columns of Z"):
        for pair in range(R // 2):
            for k in (2 * pair, 2 * pair + 1):
                zloads[k].wait()
            m = jnp.zeros((N, N), F32)
            for q in range(2 * K):
                v = zbuf[2 * pair + q // K, q % K]
                v = jnp.where(lane == col, v, 0.0)
                m += pltpu.roll(v, q * C, 1) if q else v
            merged[pair] = m.T
            for q in range(2 * K):
                at = pl.multiple_of(lax.rem(col + q, 2 * K) * C, C)
                zslot[2 * pair + q // K, q % K] = merged[pair, pl.ds(at, C), :]
        for k in range(R):
            for d in range(BAND):
                zwin[R + k, k + d] = zslot[k, zslots[k][d]]

    with jax.named_scope("entry wait"):
        pl.semaphore_wait(barrier, 5)

    def copy(src, dst, send, recv, device):
        return pltpu.make_async_remote_copy(
            src_ref=src, dst_ref=dst, send_sem=send, recv_sem=recv, device_id=device,
            device_id_type=pl.DeviceIdType.MESH,
        )

    def halo(win, stage, r):
        up = copy(
            win.at[R + r, pl.ds(R, r + R + 1)], win.at[r, pl.ds(0, r + R + 1)],
            halo_send.at[stage, 0, r], halo_recv.at[stage, 0, r], nxt,
        )
        down = copy(
            win.at[R + r, pl.ds(r, 2 * R - r)], win.at[2 * R + r, pl.ds(r + R, 2 * R - r)],
            halo_send.at[stage, 1, r], halo_recv.at[stage, 1, r], prv,
        )
        return up, down

    halos = [[halo(win, stage, r) for r in range(R)] for stage, win in enumerate((zwin, xwin, pwin))]
    for r in range(R):
        for c in halos[0][r]:
            c.start()

    with jax.named_scope("other tables"):
        hrel = [[relative(hp, i, s) for s in range(K)] for i in range(R)]
        frel = [[relative(fp, i, s) for s in range(K)] for i in range(R)]
        keep = [[(slot_at(frel, i, d) < K).astype(F32) for d in range(BAND)] for i in range(R)]

    with jax.named_scope("parts of H and Z"):
        for k in range(R):
            for s in range(K):
                hi, lo = split(zbuf[k, s])
                zsplit[k, s] = jnp.concatenate([hi, lo], 1).astype(BF16)
        for k in range(R):
            hloads[k].wait()
            for s in range(K):
                hsplit[k, s] = stacked(hbuf[k, s])

    with jax.named_scope("halo of Z wait"):
        for r in range(R):
            for c in halos[0][r]:
                c.wait_recv()

    with jax.named_scope("product W"):
        for i in range(R):
            lhs = jnp.concatenate([stacked(rows_of(zwin[hrel[i][s], i : i + BAND])) for s in range(K)], 1)
            rhs = jnp.concatenate([hsplit[i, s] for s in range(K)], 1)
            w = quadrants(dot(lhs, rhs, 1))
            for d in range(BAND):
                wband[i, i + d] = w[C * d : C * d + C] * keep[i][d]

    def part_copy(w):
        if w < R:
            n = w + R + 1
            return copy(
                part.at[w, pl.ds(0, n)], from_next.at[w, pl.ds(R, n)], part_send.at[w], part_recv.at[w], prv
            )
        r = w - 2 * R
        n = 2 * R - r
        return copy(
            part.at[w, pl.ds(r + R, n)], from_prev.at[r, pl.ds(r, n)], part_send.at[r + R], part_recv.at[r + R], nxt
        )

    parts = {w: part_copy(w) for w in (*range(R), *range(2 * R, 3 * R))}
    order = [w for r in range(R) for w in (r, 2 * R + r)] + list(range(R, 2 * R))
    with jax.named_scope("partial X"):
        for w in order:
            ks = [k for k in range(R) if 0 <= w - k < BAND]
            lo, hi = max(0, w - R), min(WIN, w + R + 1)
            lhs = jnp.concatenate([stacked(rows_of(wband[k, lo:hi])) for k in ks], 1)
            rhs = jnp.concatenate([zsplit[k, zslots[k][w - k]] for k in ks], 0)
            x = quadrants(dot(lhs, rhs, 0))
            for j in range(lo, hi):
                part[w, j] = x[C * (j - lo) : C * (j - lo) + C]
            if w in parts:
                parts[w].start()

    def shard(chip_, core_, i):
        return xall.at[i, :, pl.ds(pl.multiple_of((chip_ * 2 + core_) * C, C), C), :]

    def ring(direction, dist, i):
        device = right if direction == 0 else left
        source = lax.rem(chip + (1 - dist if direction == 0 else dist - 1) + CHIPS, CHIPS)
        ref = shard(source, core, i)
        return copy(ref, ref, ring_send.at[direction, dist - 1, i], ring_recv.at[direction, dist - 1, i], device)

    def landed(direction, dist, i):
        source = lax.rem(chip + (-dist if direction == 0 else dist) + CHIPS, CHIPS)
        ref = shard(source, core, i)
        return copy(
            ref, ref, ring_send.at[direction, dist - 1, i], ring_recv.at[direction, dist - 1, i],
            right if direction == 0 else left,
        )

    def pair(offset, i, mine):
        source = lax.rem(chip + offset, CHIPS)
        ref = shard(source, core if mine else 1 - core, i)
        return copy(ref, ref, pair_send.at[offset, i], pair_recv.at[offset, i], other)

    sent = []

    def start(c):
        c.start()
        sent.append(c)

    with jax.named_scope("sum X"):
        for i in range(R):
            parts[i].wait_recv()
            parts[2 * R + i].wait_recv()
            for d in range(BAND):
                j = i + d
                x = part[R + i, j]
                if j >= R:
                    x += from_next[i, j]
                if j < 2 * R:
                    x += from_prev[i, j]
                x *= keep[i][d]
                xwin[R + i, j] = x
                xband[i, j] = x
            at = pl.ds(pl.multiple_of(col * C, C), C)
            for t in range(K):
                xall[i, t, at, :] = xband[i, frel[i][t]]
            start(ring(0, 1, i))
            start(ring(1, 1, i))
            start(pair(0, i, True))
            for c in halos[1][i]:
                c.start()

    far = CHIPS // 2

    def steps(i, dist):
        for direction in (0, 1):
            if dist == far and i % 2 != direction:
                continue
            landed(direction, dist, i).wait_recv()
            if dist < far - 1 or (dist == far - 1 and i % 2 == direction):
                start(ring(direction, dist + 1, i))
            start(pair(CHIPS - dist if direction == 0 else dist, i, True))

    with jax.named_scope("step 1"):
        for i in range(R):
            steps(i, 1)

    with jax.named_scope("halo of X wait"):
        for r in range(R):
            for c in halos[1][r]:
                c.wait_recv()

    with jax.named_scope("step 2"):
        for i in range(R):
            steps(i, 2)
            lefts[i] = jnp.concatenate([stacked(rows_of(xwin[frel[i][s], i : i + BAND])) for s in range(K)], 1)

    with jax.named_scope("step 3"):
        for i in range(R):
            steps(i, 3)

    with jax.named_scope("step 4 and product S"):
        for i in range(R):
            steps(i, 4)
            for offset in range(CHIPS):
                pair(offset, i, False).wait_recv()
            rhs = []
            for s in range(K):
                hi, lo = split(xall[i, s])
                rhs.append(jnp.concatenate([hi, lo], 1).astype(BF16))
            square = quadrants(dot(lefts[i], jnp.concatenate(rhs, 0), 0))
            for d in range(BAND):
                pwin[R + i, i + d] = 2.0 * xwin[R + i, i + d] - square[C * d : C * d + C] * keep[i][d]
            for c in halos[2][i]:
                c.start()

    with jax.named_scope("halo of P wait"):
        for r in range(R):
            for c in halos[2][r]:
                c.wait_recv()

    with jax.named_scope("product Y"):
        for i in range(R):
            lhs = jnp.concatenate([stacked(rows_of(pwin[rrel[i][s], i : i + BAND])) for s in range(K)], 1)
            rhs = jnp.concatenate(
                [jnp.concatenate([zsplit[i, s, :, :N], zsplit[i, s, :, N:]], 0) for s in range(K)], 1
            )
            y = quadrants(dot(lhs, rhs, 1))
            for d in range(BAND):
                yband[i, i + d] = y[C * d : C * d + C]
            for t in range(K):
                out[i, t] = yband[i, frel[i][t]]

    with jax.named_scope("drain"):
        for stage in range(3):
            for r in range(R):
                for c in halos[stage][r]:
                    c.wait_send()
        for c in parts.values():
            c.wait_send()
        for c in sent:
            c.wait_send()

def shards(hamiltonian, intersection_root, ham_pattern, root_pattern, filter_pattern):

    total_rows = ham_pattern.shape[0]
    hbm = pl.BlockSpec(memory_space=pltpu.HBM)
    dma = pltpu.SemaphoreType.DMA
    window = pltpu.VMEM((WIN + 1, WIN + 1, C, N), F32)
    return pl.pallas_call(
        functools.partial(kernel, total_rows),
        out_shape=jax.ShapeDtypeStruct((R, K, C, N), F32),
        in_specs=[hbm] * 5,
        out_specs=pl.BlockSpec(memory_space=pltpu.VMEM),
        scratch_shapes=[
            *[pltpu.SMEM((K, total_rows), jnp.int32)] * 3,
            pltpu.VMEM((R, K, N, N), F32),
            pltpu.VMEM((R, K, N, N), F32),
            pltpu.VMEM((R, K, 2 * N, N), BF16),
            pltpu.VMEM((R, K + 1, N, 2 * N), BF16),
            pltpu.VMEM((R // 2, N, N), F32),
            pltpu.VMEM((R, K + 1, C, N), F32),
            window,
            pltpu.VMEM((R, WIN, C, N), F32),
            pltpu.VMEM((WIN, WIN, C, N), F32),
            pltpu.VMEM((R, WIN, C, N), F32),
            pltpu.VMEM((R, WIN, C, N), F32),
            window,
            pltpu.VMEM((R, WIN + 1, C, N), F32),
            pltpu.VMEM((R, K, N, N), F32),
            pltpu.VMEM((R, 2 * BAND * C, K * N), BF16),
            window,
            pltpu.VMEM((R, WIN + 1, C, N), F32),
            dma((2, R)),
            dma((3,)),
            dma((3, 2, R)),
            dma((3, 2, R)),
            dma((2 * R,)),
            dma((2 * R,)),
            dma((2, CHIPS // 2, R)),
            dma((2, CHIPS // 2, R)),
            dma((CHIPS, R)),
            dma((CHIPS, R)),
        ],
        compiler_params=pltpu.CompilerParams(
            collective_id=0, has_side_effects=True, vmem_limit_bytes=63 * 2**20
        ),
        cost_estimate=pl.CostEstimate(flops=4 * 270_000_000, bytes_accessed=4_400_000, transcendentals=0),
    )(hamiltonian, intersection_root, ham_pattern.T, root_pattern.T, filter_pattern.T)


def solution(mesh):
    return jax.shard_map(
        shards,
        mesh=mesh,
        in_specs=(P("rows", None, None, None), P("rows", None, None, None), P(), P(), P()),
        out_specs=P("rows", None, "cols", None),
        check_vma=False,
    )
```

time: 136 us -> 60.3 us (0.44)
  Pallas kernels: 0 us -> 58.6 us
  starting transfers between devices: 52.5 us -> 0 us
  waiting for transfers between devices: 31.3 us -> 0 us
  matrix products: 16.3 us -> 0 us
  local copies, waits for them, and re-layouts: 16.8 us -> 1.57 us
  between operations: 13.8 us -> 0.01 us
  other arithmetic: 4.69 us -> 0 us
    pallas_call x0 -> x1, Pallas kernels: none -> 58.6 us  [shards(): pl.pallas_call(functools.partial(kernel, total_rows), out_shape=jax.Shape...]
    ppermute x8 -> x0, starting transfers between devices: 52.5 us -> none  [the longest x3 32.8 us: padded(): lax.ppermute(head, axis, [((i + 1) % count, i) for i in range(count)])]
    all_gather x1 -> x0, waiting for transfers between devices: 26.2 us -> none  [shards(): gathered = lax.all_gather(assembled, 'cols', axis=2, tiled=True)]
    dot_general x9 -> x0, matrix products: 16.3 us -> none  [the longest x3 4.91 us: select_right(): jnp.einsum('ksut,ksucb->kstcb', matches.astype(jnp.float32), picked, prec...]
    gather x6 -> x0, local copies, waits for them, and re-layouts: 5.39 us -> none  [the longest x3 3.07 us: select_right(): picked = row_window[position]]
    ppermute x8 -> x0, waiting for transfers between devices: 5.05 us -> none  [the longest x3 2.33 us: padded(): lax.ppermute(head, axis, [((i + 1) % count, i) for i in range(count)])]
    dynamic_slice x2 -> x0, local copies, waits for them, and re-layouts: 2.62 us -> none  [the longest x1 1.96 us: shards(): lax.dynamic_slice_in_dim(intersection_root, lax.axis_index('cols') * slic...]
    unnamed x37 -> x1, local copies, waits for them, and re-layouts: 4.11 us -> 1.57 us
  transfers between devices with their start and end apart: 9 -> 0, of which waited for: 6 -> 0; matrix products, arithmetic and copies ran while one was open for 11% -> 0% of each run, Pallas kernels for 0% -> 0%
where the time goes in v1:
time: 60.3 us; the launch traced here: 60.2 us
  Pallas kernels  58.6 us (97%)
  local copies, waits for them, and re-layouts  1.57 us (3%)
    pallas_call x1, Pallas kernels, shards(): pl.pallas_call(functools.partial(kernel, total_rows), out_shape=jax.Shape...  58.6 us
    unnamed x1, local copies, waits for them, and re-layouts  1.57 us

profile of v1, /device:TPU:1, one launch (start us, length us, event | category | flops | bytes accessed | tf_op | source)
XLA Modules:
  0.0 60.2 jit_solution(2967618773405289160)
XLA Ops:
  0.0 58.6 %shard_map.55 = f32[4,8,8,128]{3,2,1,0:T(8,128)} custom-call(f32[4,8,128,128]{3,2,1,0:T(8,128)} %h_hbm.1, f32[4,8,128,128]{3,2,1,0:T(8,128)} %z_hbm.1, s32[8,256]{1,0:T(8,128)} %bitcast.3, s32[8,256]{1,0:T(8,128)} %bitcast.4, s32[8,256]{1,0:T(8,128)} %bitcast.5), custom_call_target="tpu_custom_call" | custom-call | flops 1080000000 | bytes 4400000 | tf_op jit(solution)/shard_map/pallas_call | solution.py:327
  58.6 1.6 %copy.7 = f32[4,8,8,128]{3,2,1,0:T(8,128)} copy(f32[4,8,8,128]{3,2,1,0:T(8,128)} %shard_map.55) | data formatting | bytes 262144

commit v2 on v1

v2 whole, which is shorter than its diff:
```python
import functools

import jax
import jax.numpy as jnp
from jax import lax
from jax.experimental import pallas as pl
from jax.experimental.pallas import tpu as pltpu
from jax.sharding import PartitionSpec as P

R = 4
K = 8
N = 128
C = 8
BAND = 2 * R + 1
WIN = 3 * R
CHIPS = 8
HALF = R // 2
F32, BF16 = jnp.float32, jnp.bfloat16


def split(x):
    hi = x.astype(BF16).astype(F32)
    return hi, x - hi


def stacked(x):
    return jnp.concatenate(split(x), 0).astype(BF16)


def rows_of(tiles):
    return tiles.reshape(tiles.shape[0] * C, N)


def quadrants(x):
    half = x.shape[0] // 2
    return (x[half:, N:] + x[half:, :N]) + (x[:half, N:] + x[:half, :N])


def dot(a, b, b_dim):
    return lax.dot_general(a, b, (((1,), (b_dim,)), ((), ())), preferred_element_type=F32)


def kernel(
    total_rows, h_hbm, z_hbm, hp_hbm, rp_hbm, fp_hbm, out,
    hp, rp, fp, zbuf, hbuf, hsplit, zsplit, merged, zslot, zwin, wband, part, from_next, from_prev,
    xwin, xwin_other, xband, xslot, xall, lefts, pwin, pother, yband,
    load_sem, pat_sem, halo_send, halo_recv, part_send, part_recv, ring_send, ring_recv,
    give_send, give_recv, own_send, own_recv, pass_send, pass_recv, p_send, p_recv, p_give_recv,
):
    groups = total_rows // R
    row, col = lax.axis_index("rows"), lax.axis_index("cols")
    chip, core = col // 2, lax.rem(col, 2)
    mate = chip * 2 + (1 - core)
    first = row * R
    up, down = lax.rem(row + 1, groups), lax.rem(row + groups - 1, groups)
    nxt, prv = {"rows": up, "cols": col}, {"rows": down, "cols": col}
    nxt_other, prv_other = {"rows": up, "cols": mate}, {"rows": down, "cols": mate}
    right = {"rows": row, "cols": lax.rem(chip + 1, CHIPS) * 2 + core}
    left = {"rows": row, "cols": lax.rem(chip + CHIPS - 1, CHIPS) * 2 + core}
    other = {"rows": row, "cols": mate}

    pats = [
        pltpu.make_async_copy(a, b, pat_sem.at[i])
        for i, (a, b) in enumerate(((rp_hbm, rp), (hp_hbm, hp), (fp_hbm, fp)))
    ]
    zloads = [pltpu.make_async_copy(z_hbm.at[k], zbuf.at[k], load_sem.at[0, k]) for k in range(R)]
    hloads = [pltpu.make_async_copy(h_hbm.at[k], hbuf.at[k], load_sem.at[1, k]) for k in range(R)]
    for c in pats + zloads + hloads:
        c.start()

    for win in (zwin, xwin, xwin_other, pwin):
        for r in range(WIN + 1):
            win[r] = jnp.zeros((WIN + 1, C, N), F32)
    for k in range(R):
        wband[k] = jnp.zeros((WIN, C, N), F32)
        yband[k] = jnp.zeros((WIN + 1, C, N), F32)
        xband[k, WIN] = jnp.zeros((C, N), F32)
        zslot[k, K] = jnp.zeros((C, N), F32)
        zsplit[k, K] = jnp.zeros((N, 2 * N), BF16)
    for r in range(HALF):
        pother[r] = jnp.zeros((WIN, C, N), F32)

    barrier = pltpu.get_barrier_semaphore()
    neighbours = (nxt, prv, right, left, other, nxt_other, prv_other)
    for device in neighbours:
        pl.semaphore_signal(barrier, inc=1, device_id=device, device_id_type=pl.DeviceIdType.MESH)

    for c in pats:
        c.wait()

    def relative(pat, i, s):
        p = pat[s, first + i]
        v = p - first + R
        v = jnp.where(v < 0, v + total_rows, v)
        v = jnp.where(v >= total_rows, v - total_rows, v)
        return jnp.where(p < 0, WIN, jnp.minimum(v, WIN))

    def slot_at(rel, i, d):
        slot = jnp.int32(K)
        for s in range(K):
            slot = jnp.where(rel[s] == i + d, s, slot)
        return slot

    def kept(rel, i):
        return [(slot_at(rel, i, d) < K).astype(F32) for d in range(BAND)]

    rrel = [[relative(rp, i, s) for s in range(K)] for i in range(R)]
    zslots = [[slot_at(rrel[i], i, d) for d in range(BAND)] for i in range(R)]

    def copy(src, dst, send, recv, device):
        return pltpu.make_async_remote_copy(
            src_ref=src, dst_ref=dst, send_sem=send, recv_sem=recv, device_id=device,
            device_id_type=pl.DeviceIdType.MESH,
        )

    sent = []

    def start(c):
        c.start()
        sent.append(c)

    def halo(win, stage, r):
        ahead = copy(
            win.at[R + r, pl.ds(R, r + R + 1)], win.at[r, pl.ds(0, r + R + 1)],
            halo_send.at[stage, 0, r], halo_recv.at[stage, 0, r], nxt,
        )
        back = copy(
            win.at[R + r, pl.ds(r, 2 * R - r)], win.at[2 * R + r, pl.ds(r + R, 2 * R - r)],
            halo_send.at[stage, 1, r], halo_recv.at[stage, 1, r], prv,
        )
        return ahead, back

    halos = [[halo(win, stage, r) for r in range(R)] for stage, win in enumerate((zwin, xwin))]

    lane = lax.broadcasted_iota(jnp.int32, (N, N), 1) // C
    for pair in range(R // 2):
        rows = (2 * pair, 2 * pair + 1)
        for k in rows:
            zloads[k].wait()
        m = jnp.zeros((N, N), F32)
        for q in range(2 * K):
            v = zbuf[2 * pair + q // K, q % K]
            v = jnp.where(lane == col, v, 0.0)
            m += pltpu.roll(v, q * C, 1) if q else v
        merged[pair] = m.T
        for q in range(2 * K):
            at = pl.multiple_of(lax.rem(col + q, 2 * K) * C, C)
            zslot[2 * pair + q // K, q % K] = merged[pair, pl.ds(at, C), :]
        for k in rows:
            for d in range(BAND):
                zwin[R + k, k + d] = zslot[k, zslots[k][d]]
        if pair == 0:
            pl.semaphore_wait(barrier, len(neighbours))
        for k in rows:
            for c in halos[0][k]:
                start(c)

    hrel = [[relative(hp, i, s) for s in range(K)] for i in range(R)]
    frel = [[relative(fp, i, s) for s in range(K)] for i in range(R)]
    keep = [kept(frel[i], i) for i in range(R)]
    mine = [core * HALF + r for r in range(HALF)]
    mine_rel = [[relative(fp, i, s) for s in range(K)] for i in mine]
    mine_keep = [kept(rel, i) for rel, i in zip(mine_rel, mine)]
    for k in range(R):
        for s in range(K):
            hi, lo = split(zbuf[k, s])
            zsplit[k, s] = jnp.concatenate([hi, lo], 1).astype(BF16)
    for k in range(R):
        hloads[k].wait()
        for s in range(K):
            hsplit[k, s] = stacked(hbuf[k, s])
    for r in range(R):
        for c in halos[0][r]:
            c.wait_recv()

    for i in range(R):
        lhs = jnp.concatenate([stacked(rows_of(zwin[hrel[i][s], i : i + BAND])) for s in range(K)], 1)
        rhs = jnp.concatenate([hsplit[i, s] for s in range(K)], 1)
        w = quadrants(dot(lhs, rhs, 1))
        for d in range(BAND):
            wband[i, i + d] = w[C * d : C * d + C] * keep[i][d]

    def part_copy(w):
        if w < R:
            n = w + R + 1
            return copy(
                part.at[w, pl.ds(0, n)], from_next.at[w, pl.ds(R, n)], part_send.at[w], part_recv.at[w], prv
            )
        r = w - 2 * R
        n = 2 * R - r
        return copy(
            part.at[w, pl.ds(r + R, n)], from_prev.at[r, pl.ds(r, n)], part_send.at[r + R], part_recv.at[r + R], nxt
        )

    parts = {w: part_copy(w) for w in (*range(R), *range(2 * R, 3 * R))}
    order = [w for r in range(R) for w in (r, 2 * R + r)] + list(range(R, 2 * R))
    for w in order:
        ks = [k for k in range(R) if 0 <= w - k < BAND]
        lo, hi = max(0, w - R), min(WIN, w + R + 1)
        lhs = jnp.concatenate([stacked(rows_of(wband[k, lo:hi])) for k in ks], 1)
        rhs = jnp.concatenate([zsplit[k, zslots[k][w - k]] for k in ks], 0)
        x = quadrants(dot(lhs, rhs, 0))
        for j in range(lo, hi):
            part[w, j] = x[C * (j - lo) : C * (j - lo) + C]
        if w in parts:
            start(parts[w])

    def ring(direction, dist, r, theirs, source, src=None):
        ref = xall.at[r, source * 2 + (1 - core if theirs else core)]
        piece = 2 * r + theirs
        return copy(
            ref if src is None else src, ref, ring_send.at[direction, dist - 1, piece],
            ring_recv.at[direction, dist - 1, piece], left if direction else right,
        )

    def give(r):
        return copy(xslot.at[(1 - core) * HALF + r], xall.at[r, col], give_send.at[r], give_recv.at[r], other)

    def given(r):
        return copy(xslot.at[r], xall.at[r, mate], give_send.at[r], give_recv.at[r], other)

    for i in range(R):
        parts[i].wait_recv()
        parts[2 * R + i].wait_recv()
        for d in range(BAND):
            j = i + d
            x = part[R + i, j]
            if j >= R:
                x += from_next[i, j]
            if j < 2 * R:
                x += from_prev[i, j]
            x *= keep[i][d]
            xwin[R + i, j] = x
            xband[i, j] = x
        for t in range(K):
            xslot[i, t] = xband[i, frel[i][t]]

        @pl.when(core == i // HALF)
        def _():
            for direction in (0, 1):
                ring(direction, 1, i % HALF, 0, chip, xslot.at[i]).start()

        @pl.when(core != i // HALF)
        def _():
            give(i % HALF).start()

        if i % HALF == HALF - 1 and i > HALF:
            for r in range(HALF):
                given(r).wait_recv()
                for direction in (0, 1):
                    start(ring(direction, 1, r, 1, chip))

    for r in range(HALF):
        sent += [give(r)] + [ring(direction, 1, r, 0, chip, xslot.at[r]) for direction in (0, 1)]

    def own_row(i):
        ref = (R + i, pl.ds(i, BAND))
        return copy(xwin.at[ref], xwin_other.at[ref], own_send.at[i], own_recv.at[i], other)

    def pass_on(direction, r):
        ref = (r, pl.ds(0, r + R + 1)) if direction == 0 else (2 * R + r, pl.ds(r + R, 2 * R - r))
        return copy(xwin.at[ref], xwin_other.at[ref], pass_send.at[direction, r], pass_recv.at[direction, r], other)

    for i in range(R):
        for c in halos[1][i]:
            start(c)
        start(own_row(i))
    for r in range(HALF):
        xall[r, col] = xslot[mine[r]]

    far = CHIPS // 2

    def steps(r, dist):
        for theirs in (0, 1):
            for direction in (0, 1):
                turn = (r + theirs) % 2 == direction
                if dist == far and not turn:
                    continue
                source = lax.rem(chip + (dist if direction else -dist) + CHIPS, CHIPS)
                ring(direction, dist, r, theirs, source).wait_recv()
                if dist < far - 1 or (dist == far - 1 and turn):
                    start(ring(direction, dist + 1, r, theirs, source))

    for r in range(HALF):
        steps(r, 1)
    for r in range(HALF):
        steps(r, 2)
    for r in range(R):
        for direction, c in enumerate(halos[1][r]):
            c.wait_recv()
            start(pass_on(direction, r))

    def windows(r):
        at = pl.ds(mine[r], BAND)
        lefts[r] = jnp.concatenate(
            [
                stacked(rows_of(jnp.concatenate([win[mine_rel[r][s], at] for win in (xwin, xwin_other)], 0)))
                for s in range(K)
            ],
            1,
        )

    def p_copies(r):
        i = mine[r]
        ahead, back = R + HALF + r + 1, 2 * R - r
        copies = []
        for theirs, (n, p) in enumerate(((nxt, prv), (nxt_other, prv_other))):
            src = pother.at[r] if theirs else pwin.at[R + i]
            copies.append(
                copy(
                    src.at[pl.ds(R, ahead)], pwin.at[i, pl.ds(0, ahead)],
                    p_send.at[r, theirs, 0], p_recv.at[0, i], n,
                )
            )
            copies.append(
                copy(
                    src.at[pl.ds(r, back)], pwin.at[2 * R + i, pl.ds(R + r, back)],
                    p_send.at[r, theirs, 1], p_recv.at[1, i], p,
                )
            )
        ref = pl.ds(i, BAND)
        copies.append(
            copy(pother.at[r, ref], pwin.at[R + i, ref], p_send.at[r, 2, 0], p_give_recv.at[r], other)
        )
        return copies

    steps(0, 3)
    steps(1, 3)
    for r in range(R):
        own_row(r).wait_recv()
        for direction in (0, 1):
            pass_on(direction, r).wait_recv()
    windows(0)
    windows(1)
    for r in range(HALF):
        steps(r, 4)
        i = mine[r]
        rhs = []
        for s in range(K):
            hi, lo = split(rows_of(xall[r, :, s]))
            rhs.append(jnp.concatenate([hi, lo], 1).astype(BF16))
        square = quadrants(dot(lefts[r], jnp.concatenate(rhs, 0), 0))
        for d in range(BAND):
            s0, s1 = (square[C * e : C * e + C] * mine_keep[r][d] for e in (d, BAND + d))
            pwin[R + i, i + d] = 2.0 * xwin[R + i, i + d] - s0
            pother[r, i + d] = 2.0 * xwin_other[R + i, i + d] - s1
        for c in p_copies(r):
            start(c)

    for r in range(R):
        ahead, back = R + HALF + r % HALF + 1, 2 * R - r % HALF
        ref = pwin.at[r, pl.ds(0, ahead)]
        copy(ref, ref, p_send.at[0, 0, 0], p_recv.at[0, r], nxt).wait_recv()
        ref = pwin.at[2 * R + r, pl.ds(R + r % HALF, back)]
        copy(ref, ref, p_send.at[0, 0, 1], p_recv.at[1, r], prv).wait_recv()
    for r in range(HALF):
        i = (1 - core) * HALF + r
        ref = pwin.at[R + i, pl.ds(i, BAND)]
        copy(ref, ref, p_send.at[r, 2, 0], p_give_recv.at[r], other).wait_recv()

    for i in range(R):
        lhs = jnp.concatenate([stacked(rows_of(pwin[rrel[i][s], i : i + BAND])) for s in range(K)], 1)
        rhs = jnp.concatenate(
            [jnp.concatenate([zsplit[i, s, :, :N], zsplit[i, s, :, N:]], 0) for s in range(K)], 1
        )
        y = quadrants(dot(lhs, rhs, 1))
        for d in range(BAND):
            yband[i, i + d] = y[C * d : C * d + C]
        for t in range(K):
            out[i, t] = yband[i, frel[i][t]]

    for c in sent:
        c.wait_send()


def shards(hamiltonian, intersection_root, ham_pattern, root_pattern, filter_pattern):

    total_rows = ham_pattern.shape[0]
    hbm = pl.BlockSpec(memory_space=pltpu.HBM)
    dma = pltpu.SemaphoreType.DMA
    window = pltpu.VMEM((WIN + 1, WIN + 1, C, N), F32)
    return pl.pallas_call(
        functools.partial(kernel, total_rows),
        out_shape=jax.ShapeDtypeStruct((R, K, C, N), F32),
        in_specs=[hbm] * 5,
        out_specs=pl.BlockSpec(memory_space=pltpu.VMEM),
        scratch_shapes=[
            *[pltpu.SMEM((K, total_rows), jnp.int32)] * 3,
            pltpu.VMEM((R, K, N, N), F32),
            pltpu.VMEM((R, K, N, N), F32),
            pltpu.VMEM((R, K, 2 * N, N), BF16),
            pltpu.VMEM((R, K + 1, N, 2 * N), BF16),
            pltpu.VMEM((R // 2, N, N), F32),
            pltpu.VMEM((R, K + 1, C, N), F32),
            window,
            pltpu.VMEM((R, WIN, C, N), F32),
            pltpu.VMEM((WIN, WIN, C, N), F32),
            pltpu.VMEM((R, WIN, C, N), F32),
            pltpu.VMEM((R, WIN, C, N), F32),
            window,
            window,
            pltpu.VMEM((R, WIN + 1, C, N), F32),
            pltpu.VMEM((R, K, C, N), F32),
            pltpu.VMEM((HALF, 2 * CHIPS, K, C, N), F32),
            pltpu.VMEM((HALF, 4 * BAND * C, K * N), BF16),
            window,
            pltpu.VMEM((HALF, WIN, C, N), F32),
            pltpu.VMEM((R, WIN + 1, C, N), F32),
            dma((2, R)),
            dma((3,)),
            *[dma((2, 2, R))] * 2,
            *[dma((2 * R,))] * 2,
            *[dma((2, CHIPS // 2, 2 * HALF))] * 2,
            *[dma((HALF,))] * 2,
            *[dma((R,))] * 2,
            *[dma((2, R))] * 2,
            dma((HALF, 3, 2)),
            dma((2, R)),
            dma((HALF,)),
        ],
        compiler_params=pltpu.CompilerParams(
            collective_id=0, has_side_effects=True, vmem_limit_bytes=63 * 2**20
        ),
        cost_estimate=pl.CostEstimate(flops=4 * 270_000_000, bytes_accessed=4_400_000, transcendentals=0),
    )(hamiltonian, intersection_root, ham_pattern.T, root_pattern.T, filter_pattern.T)


def solution(mesh):
    return jax.shard_map(
        shards,
        mesh=mesh,
        in_specs=(P("rows", None, None, None), P("rows", None, None, None), P(), P(), P()),
        out_specs=P("rows", None, "cols", None),
        check_vma=False,
    )
```

time: 60.3 us -> 59.2 us (0.982)
  Pallas kernels: 58.6 us -> 57.4 us
    pallas_call x1, Pallas kernels: 58.6 us -> 57.4 us  [shards(): pl.pallas_call(functools.partial(kernel, total_rows), out_shape=jax.Shape...]
where the time goes in v2:
time: 59.2 us; the launch traced here: 59 us
  Pallas kernels  57.4 us (97%)
  local copies, waits for them, and re-layouts  1.57 us (3%)
    pallas_call x1, Pallas kernels, shards(): pl.pallas_call(functools.partial(kernel, total_rows), out_shape=jax.Shape...  57.4 us
    unnamed x1, local copies, waits for them, and re-layouts  1.57 us

profile of v2, /device:TPU:1, one launch (start us, length us, event | category | flops | bytes accessed | tf_op | source)
XLA Modules:
  0.0 59.0 jit_solution(12873181952581528738)
XLA Ops:
  0.0 57.4 %shard_map.55 = f32[4,8,8,128]{3,2,1,0:T(8,128)} custom-call(f32[4,8,128,128]{3,2,1,0:T(8,128)} %h_hbm.1, f32[4,8,128,128]{3,2,1,0:T(8,128)} %z_hbm.1, s32[8,256]{1,0:T(8,128)} %bitcast.3, s32[8,256]{1,0:T(8,128)} %bitcast.4, s32[8,256]{1,0:T(8,128)} %bitcast.5), custom_call_target="tpu_custom_call" | custom-call | flops 1080000000 | bytes 4400000 | tf_op jit(solution)/shard_map/pallas_call | solution.py:382
  57.4 1.6 %copy.7 = f32[4,8,8,128]{3,2,1,0:T(8,128)} copy(f32[4,8,8,128]{3,2,1,0:T(8,128)} %shard_map.55) | data formatting | bytes 262144

commit v3 on v2

--- a/solution.py
+++ b/solution.py
@@ -57,6 +57,8 @@
     nxt_other, prv_other = {"rows": up, "cols": mate}, {"rows": down, "cols": mate}
     right = {"rows": row, "cols": lax.rem(chip + 1, CHIPS) * 2 + core}
     left = {"rows": row, "cols": lax.rem(chip + CHIPS - 1, CHIPS) * 2 + core}
+    right2 = {"rows": row, "cols": lax.rem(chip + 2, CHIPS) * 2 + core}
+    left2 = {"rows": row, "cols": lax.rem(chip + CHIPS - 2, CHIPS) * 2 + core}
     other = {"rows": row, "cols": mate}
 
     pats = [
@@ -81,7 +83,7 @@
         pother[r] = jnp.zeros((WIN, C, N), F32)
 
     barrier = pltpu.get_barrier_semaphore()
-    neighbours = (nxt, prv, right, left, other, nxt_other, prv_other)
+    neighbours = (nxt, prv, right, left, right2, left2, other, nxt_other, prv_other)
     for device in neighbours:
         pl.semaphore_signal(barrier, inc=1, device_id=device, device_id_type=pl.DeviceIdType.MESH)
 
@@ -205,12 +207,14 @@
         if w in parts:
             start(parts[w])
 
+    far = CHIPS // 2
+
     def ring(direction, dist, r, theirs, source, src=None):
         ref = xall.at[r, source * 2 + (1 - core if theirs else core)]
         piece = 2 * r + theirs
         return copy(
             ref if src is None else src, ref, ring_send.at[direction, dist - 1, piece],
-            ring_recv.at[direction, dist - 1, piece], left if direction else right,
+            ring_recv.at[direction, dist - 1, piece], (left2, right2, left, right)[2 * (dist % 2) + (not direction)],
         )
 
     def give(r):
@@ -237,8 +241,9 @@
 
         @pl.when(core == i // HALF)
         def _():
-            for direction in (0, 1):
-                ring(direction, 1, i % HALF, 0, chip, xslot.at[i]).start()
+            for dist in (2, 1):
+                for direction in (0, 1):
+                    ring(direction, dist, i % HALF, 0, chip, xslot.at[i]).start()
 
         @pl.when(core != i // HALF)
         def _():
@@ -247,11 +252,12 @@
         if i % HALF == HALF - 1 and i > HALF:
             for r in range(HALF):
                 given(r).wait_recv()
-                for direction in (0, 1):
-                    start(ring(direction, 1, r, 1, chip))
-
-    for r in range(HALF):
-        sent += [give(r)] + [ring(direction, 1, r, 0, chip, xslot.at[r]) for direction in (0, 1)]
+                for dist in (2, 1):
+                    for direction in (0, 1):
+                        start(ring(direction, dist, r, 1, chip))
+
+    for r in range(HALF):
+        sent += [give(r)] + [ring(direction, dist, r, 0, chip, xslot.at[r]) for direction in (0, 1) for dist in (1, 2)]
 
     def own_row(i):
         ref = (R + i, pl.ds(i, BAND))
@@ -267,8 +273,6 @@
         start(own_row(i))
     for r in range(HALF):
         xall[r, col] = xslot[mine[r]]
-
-    far = CHIPS // 2
 
     def steps(r, dist):
         for theirs in (0, 1):
@@ -278,13 +282,15 @@
                     continue
                 source = lax.rem(chip + (dist if direction else -dist) + CHIPS, CHIPS)
                 ring(direction, dist, r, theirs, source).wait_recv()
-                if dist < far - 1 or (dist == far - 1 and turn):
-                    start(ring(direction, dist + 1, r, theirs, source))
-
+                if dist == 2:
+                    if turn:
+                        start(ring(direction, far, r, theirs, source))
+                    start(ring(direction, 3, r, theirs, source))
+
+    for r in range(HALF):
+        steps(r, 2)
     for r in range(HALF):
         steps(r, 1)
-    for r in range(HALF):
-        steps(r, 2)
     for r in range(R):
         for direction, c in enumerate(halos[1][r]):
             c.wait_recv()

time: 59.2 us -> 58.4 us (0.986)
  Pallas kernels: 57.4 us -> 56.7 us
    pallas_call x1, Pallas kernels: 57.4 us -> 56.7 us  [shards(): pl.pallas_call(functools.partial(kernel, total_rows), out_shape=jax.Shape...]
where the time goes in v3:
time: 58.4 us; the launch traced here: 58.2 us
  Pallas kernels  56.7 us (97%)
  local copies, waits for them, and re-layouts  1.57 us (3%)
    pallas_call x1, Pallas kernels, shards(): pl.pallas_call(functools.partial(kernel, total_rows), out_shape=jax.Shape...  56.7 us
    unnamed x1, local copies, waits for them, and re-layouts  1.57 us

profile of v3, /device:TPU:1, one launch (start us, length us, event | category | flops | bytes accessed | tf_op | source)
XLA Modules:
  0.0 58.2 jit_solution(1591143915286163457)
XLA Ops:
  0.0 56.7 %shard_map.55 = f32[4,8,8,128]{3,2,1,0:T(8,128)} custom-call(f32[4,8,128,128]{3,2,1,0:T(8,128)} %h_hbm.1, f32[4,8,128,128]{3,2,1,0:T(8,128)} %z_hbm.1, s32[8,256]{1,0:T(8,128)} %bitcast.3, s32[8,256]{1,0:T(8,128)} %bitcast.4, s32[8,256]{1,0:T(8,128)} %bitcast.5), custom_call_target="tpu_custom_call" | custom-call | flops 1080000000 | bytes 4400000 | tf_op jit(solution)/shard_map/pallas_call | solution.py:388
  56.7 1.6 %copy.7 = f32[4,8,8,128]{3,2,1,0:T(8,128)} copy(f32[4,8,8,128]{3,2,1,0:T(8,128)} %shard_map.55) | data formatting | bytes 262144

commit v4 on v3

--- a/solution.py
+++ b/solution.py
@@ -67,7 +67,7 @@
     ]
     zloads = [pltpu.make_async_copy(z_hbm.at[k], zbuf.at[k], load_sem.at[0, k]) for k in range(R)]
     hloads = [pltpu.make_async_copy(h_hbm.at[k], hbuf.at[k], load_sem.at[1, k]) for k in range(R)]
-    for c in pats + zloads + hloads:
+    for c in pats + zloads:
         c.start()
 
     for win in (zwin, xwin, xwin_other, pwin):
@@ -139,6 +139,9 @@
         rows = (2 * pair, 2 * pair + 1)
         for k in rows:
             zloads[k].wait()
+        if pair == R // 2 - 1:
+            for c in hloads:
+                c.start()
         m = jnp.zeros((N, N), F32)
         for q in range(2 * K):
             v = zbuf[2 * pair + q // K, q % K]

time: 58.4 us -> 58.4 us (level)
  no operation moved by 1% of the time
where the time goes in v4:
time: 58.4 us; the launch traced here: 58.2 us
  Pallas kernels  56.7 us (97%)
  local copies, waits for them, and re-layouts  1.57 us (3%)
    pallas_call x1, Pallas kernels, shards(): pl.pallas_call(functools.partial(kernel, total_rows), out_shape=jax.Shape...  56.7 us
    unnamed x1, local copies, waits for them, and re-layouts  1.57 us

profile of v4, /device:TPU:1, one launch (start us, length us, event | category | flops | bytes accessed | tf_op | source)
XLA Modules:
  0.0 58.2 jit_solution(436583898539897445)
XLA Ops:
  0.0 56.7 %shard_map.55 = f32[4,8,8,128]{3,2,1,0:T(8,128)} custom-call(f32[4,8,128,128]{3,2,1,0:T(8,128)} %h_hbm.1, f32[4,8,128,128]{3,2,1,0:T(8,128)} %z_hbm.1, s32[8,256]{1,0:T(8,128)} %bitcast.3, s32[8,256]{1,0:T(8,128)} %bitcast.4, s32[8,256]{1,0:T(8,128)} %bitcast.5), custom_call_target="tpu_custom_call" | custom-call | flops 1080000000 | bytes 4400000 | tf_op jit(solution)/shard_map/pallas_call | solution.py:391
  56.7 1.6 %copy.7 = f32[4,8,8,128]{3,2,1,0:T(8,128)} copy(f32[4,8,8,128]{3,2,1,0:T(8,128)} %shard_map.55) | data formatting | bytes 262144
